TPU v7x, 128 devices: a whole 4x4x4 slice. The times are simulated.
128 devices in a mesh: dp: 32 (over z, y, core), tp: 4 (over x).
Axes of the slice: x: 4, y: 4, z: 4, core: 2. Of those that a mesh axis runs over, the one named last changes fastest.
Arguments:
- queries: bfloat16 [4096, 36864], P('dp', 'tp'), may hold values from -32 to 32
- latents: bfloat16 [4096, 576], P(('dp', 'tp')), may hold values from -32 to 32
- segment_ids: int32 [4096], P('dp'), may hold values from 0 to 3, never falling along the last dimension, each value on 1 to 2048 neighbouring positions
- value_weight: bfloat16 [64, 512, 128], P('tp', 'dp'), may hold values from -0.25 to 0.25
Outputs:
- attended: bfloat16 [4096, 8192], P('dp', 'tp')
Inputs may be any that keep to these rules, and one draw needn't show every extreme that they name: `segment_ids`: ids never fall along the pack; each document holds 1 to 2048 tokens and one holds exactly 2048.
All inputs are finite; a program needn't handle non-finite values.
Results may differ from a plain program's by a relative error of at most 0.0055.
Values may be sent and summed in bfloat16 or wider, within the bound.
A program may use at most 192 MiB of HBM per device.

v0:
```python
import jax
import jax.numpy as jnp
from jax import lax
from jax.sharding import PartitionSpec as P

LATENT = 512
ROPE = 64
VALUE = 128


score_scale = 192.0 ** (-0.5)
masked_value = -1e30


def per_device(queries, latents, segment_ids, value_weight):
    row_count = queries.shape[0]
    feature_width = LATENT + ROPE
    head_count = queries.shape[1] // feature_width
    local_latent = lax.all_gather(latents, "tp", axis=0, tiled=True)
    anchor = lax.axis_index("dp") * row_count
    row_numbers = jnp.arange(row_count, dtype=jnp.int32)
    held_queries, held_ids = (queries, segment_ids)
    held_position = anchor + row_numbers
    query_rows = held_queries.reshape(row_count * head_count, feature_width)
    query_position = jnp.repeat(held_position, head_count)
    query_ids = jnp.repeat(held_ids, head_count)
    total_rows = row_count * head_count
    key_rows = lax.all_gather(local_latent, "dp", axis=0, tiled=True)
    key_position = jnp.arange(key_rows.shape[0], dtype=jnp.int32)
    allowed = (
        (query_ids[:, None] == lax.all_gather(segment_ids, "dp", axis=0, tiled=True)[None, :])
        & (key_position[None, :] <= query_position[:, None])
        & (key_position[None, :] >= 0)
    )
    highest = jnp.full((total_rows,), masked_value, jnp.float32)
    scores = (
        jnp.einsum("rd,kd->rk", query_rows, key_rows, preferred_element_type=jnp.float32)
        * score_scale
    )
    scores = jnp.where(allowed, scores, masked_value)
    new_highest = jnp.maximum(highest, jnp.max(scores, axis=1))
    weights = jnp.where(allowed, jnp.exp(scores - new_highest[:, None]), 0.0)
    weight_sum = jnp.sum(weights, axis=1)
    numerator = jnp.dot(
        weights.astype(jnp.bfloat16), key_rows[:, :LATENT], preferred_element_type=jnp.float32
    )
    running = (new_highest, weight_sum, numerator)
    highest, weight_sum, numerator = running
    context = (
        (numerator / weight_sum[:, None])
        .astype(jnp.bfloat16)
        .reshape(row_count, head_count, LATENT)
    )
    projected = jnp.einsum(
        "thc,hcv->thv",
        context,
        lax.all_gather(value_weight, "dp", axis=1, tiled=True),
        preferred_element_type=jnp.float32,
    )
    return projected.astype(jnp.bfloat16).reshape(row_count, head_count * VALUE)


def solution(mesh):
    placed = (P("dp", "tp"), P(("dp", "tp"), None), P("dp"), P("tp", "dp", None))
    return jax.shard_map(
        per_device, mesh=mesh, in_specs=placed, out_specs=P("dp", "tp"), check_vma=False
    )
```

profile of v0, /device:TPU:32, one launch (start us, length us, event | category | flops | bytes accessed | tf_op | source)
XLA Modules:
  0.0 138.3 jit_solution(14484226484147308578)
XLA Ops:
  6.5 0.0 all-gather.4.cloned.1.call-start
  6.5 13.9 %all_gather.13 = bf16[128,576]{1,0:T(8,128)(2,1)} all-gather(bf16[32,576]{1,0:T(8,128)(2,1)} %param.5), channel_id=1, replica_groups=mesh['dp'=32,'tp'=4] {'tp'}, dimensions={0}, use_global_device_ids=true | all-gather | bytes 184320 | tf_op jit(solution)/shard_map/all_gather | solution.py:19
  20.4 0.0 all-gather.4.cloned.1.call-update
  20.5 0.0 all-gather.6.cloned.1.call-start
  20.5 0.7 all-gather.6.cloned.1.call-update
  21.2 0.1 broadcast_in_dim.22
  21.3 0.1 le.16
  21.4 0.7 broadcast_in_dim.21
  22.1 0.1 eq.15
  22.2 22.3 %all-gather = s32[32,1,128]{2,1,0:T(1,128)S(1)} all-gather(s32[1,1,128]{2,1,0:T(1,128)} %bitcast.13), channel_id=1, replica_groups=mesh['dp'=32,'tp'=4] {'dp'}, dimensions={0}, use_global_device_ids=true | all-gather | bytes 16896 | tf_op jit(solution)/shard_map/all_gather | solution.py:31
  44.5 3.9 %reshape.16 = bf16[2048,576]{1,0:T(8,128)(2,1)S(1)} reshape(bf16[128,9216]{1,0:T(8,128)(2,1)} %param.4) | data formatting | bytes 4718592 | tf_op jit(solution)/shard_map/reshape | solution.py:24
  48.5 20.2 %all-gather.4.cloned.1.call-done = bf16[4096,576]{1,0:T(8,128)(2,1)} async-done(((bf16[128,576]{1,0:T(8,128)(2,1)}), bf16[4096,576]{1,0:T(8,128)(2,1)}) %all-gather.4.cloned.1.call-update) | async-done | bytes 4718608 | tf_op jit(solution)/shard_map/all_gather | solution.py:28
  68.7 23.0 %fusion.1 = (f32[2048]{0:T(1024)S(1)}, f32[2048,4096]{1,0:T(8,128)}) fusion(s32[2048]{0:T(1024)S(1)} %le.16, s32[4096]{0:T(1024)S(1)} %bitcast.10, s32[2048]{0:T(1024)S(1)} %eq.15, bf16[2048,576]{1,0:T(8,128)(2,1)S(1)} %reshape.16, bf16[4096,576]{1,0:T(8,128)(2,1)} %all-gather.4.cloned.1.call-done), kind=kOutput, calls=%fused_computation.4 | convolution fusion | flops 9714006016 | bytes 40673280 | tf_op jit(solution)/shard_map/rd,kd->rk/dot_general | solution.py:37
  91.7 0.0 slice-start
  91.7 0.0 slice-start.1
  91.7 17.1 %fusion.2 = f32[2048]{0:T(1024)S(1)} fusion(f32[2048,4096]{1,0:T(8,128)} %get-tuple-element.6, f32[2048]{0:T(1024)S(1)} %broadcast_maximum_fusion, s32[2048]{0:T(1024)S(1)} %le.16, s32[4096]{0:T(1024)S(1)} %bitcast.11, s32[2048]{0:T(1024)S(1)} %eq.15), kind=kLoop, calls=%fused_computation.5 | loop fusion | flops 67106816 | bytes 33603584 | tf_op jit(solution)/shard_map/reduce_sum | solution.py:43
  108.8 0.0 slice-done
  108.8 0.0 slice-done.1
  108.9 17.3 %divide_convert_fusion = bf16[2048,512]{1,0:T(8,128)(2,1)S(1)} fusion(f32[2048]{0:T(1024)S(1)} %fusion.2, bf16[4096,576]{1,0:T(8,128)(2,1)S(1)} %bitcast.15, f32[2048,4096]{1,0:T(8,128)} %get-tuple-element.6, f32[2048]{0:T(1024)S(1)} %broadcast_maximum_fusion, s32[2048]{0:T(1024)S(1)} %le.16, s32[4096]{0:T(1024)S(1)} %bitcast.12, s32[2048]{0:T(1024)S(1)} %eq.15), kind=kOutput, calls=%fused_computation.9 | convolution fusion | flops 8659140608 | bytes 39895040 | tf_op jit(solution)/shard_map/dot_general | solution.py:44
  126.2 0.0 all-gather.6.cloned.1.call-done
  126.2 4.3 %fusion.13 = bf16[16,128,128]{1,2,0:T(8,128)(2,1)S(1)} fusion(bf16[16,512,128]{2,1,0:T(8,128)(2,1)} %all-gather.6.cloned.1.call-done, bf16[128,16,512]{2,1,0:T(8,128)(2,1)S(1)} %bitcast.16), kind=kOutput, calls=%fused_computation.12 | convolution fusion | flops 268697600 | bytes 4718592 | tf_op jit(solution)/shard_map/thc,hcv->thv/dot_general | solution.py:54
  130.5 1.0 copy.10
  (3 shorter events, 0.0 us)
Async XLA Ops:
  6.5 62.1 %all-gather.4.cloned.1.call-start = ((), (), s32[]{:S(2)}) async-start(), calls=%async_computation | async-start | bytes 5406720 | tf_op jit(solution)/shard_map/all_gather | solution.py:28
  20.5 105.7 %all-gather.6.cloned.1.call-start = ((), (), s32[]{:S(2)}) async-start(), calls=%async_computation.1 | async-start | bytes 2162688 | tf_op jit(solution)/shard_map/all_gather | solution.py:57
  91.7 17.1 %slice-start = ((s8[5242880]{0:T(1024)(128)(4,1)}), s8[4194304]{0:T(1024)(128)(4,1)S(1)}, s32[]{:S(2)}) async-start(s8[5242880]{0:T(1024)(128)(4,1)} %bitcast.14), calls=%async_computation.2 | async-start | bytes 8388608
  91.7 17.1 %slice-start.1 = ((s8[5242880]{0:T(1024)(128)(4,1)}), s8[1048576]{0:T(1024)(128)(4,1)S(1)}, s32[]{:S(2)}) async-start(s8[5242880]{0:T(1024)(128)(4,1)} %bitcast.14), calls=%async_computation.3 | async-start | bytes 2097152
Sparse Core Ops, SparseCore 0:
  20.6 48.0 all-gather.3
  70.8 44.1 all-gather.5
where the time goes:
time: 141 us; the launch traced here: 138 us
  matrix products  44.6 us (32%)
  blocking collectives  36.2 us (26%)
  waiting for transfers between devices  20.9 us (15%)
  other arithmetic  17.1 us (12%)
  between operations  13.5 us (10%)
  local copies, waits for them, and re-layouts  5.92 us (4%)
    dot_general x1, matrix products, per_device(): jnp.einsum('rd,kd->rk', query_rows, key_rows, preferred_element_type=jnp....  23 us
    all_gather x1, blocking collectives, per_device(): lax.all_gather(segment_ids, 'dp', axis=0, tiled=True)[None, :]  22.3 us
    all_gather x1, waiting for transfers between devices, per_device(): key_rows = lax.all_gather(local_latent, 'dp', axis=0, tiled=True)  20.2 us
    dot_general x1, matrix products, per_device(): jnp.dot(weights.astype(jnp.bfloat16), key_rows[:, :LATENT], preferred_ele...  17.3 us
    reduce_sum x1, other arithmetic, per_device(): weight_sum = jnp.sum(weights, axis=1)  17.1 us
    all_gather x1, blocking collectives, per_device(): local_latent = lax.all_gather(latents, 'tp', axis=0, tiled=True)  13.9 us
    dot_general x1, matrix products, per_device(): jnp.einsum('thc,hcv->thv', context, lax.all_gather(value_weight, 'dp', ax...  4.26 us
    reshape x1, local copies, waits for them, and re-layouts, per_device(): query_rows = held_queries.reshape(row_count * head_count, feature_width)  3.92 us
  transfers between devices with their start and end apart: 2, of which 1 were waited for; matrix products, arithmetic and copies ran while one was open for 45% of the time, Pallas kernels for 0%

commit v1 on v0

v1 whole, which is shorter than its diff:
```python
import functools

import jax
import jax.numpy as jnp
from jax import lax
from jax.experimental import pallas as pl
from jax.experimental.pallas import tpu as pltpu
from jax.sharding import PartitionSpec as P

MESH = pl.DeviceIdType.MESH
F32, BF16 = jnp.float32, jnp.bfloat16
LATENT, ROPE, VALUE = 512, 64, 128
FEAT = LATENT + ROPE
WIDE = 640
TOK = 128
HEADS = 16
ROWS = TOK * HEADS
CHUNK = 2 * TOK
NCH = 9
SHARD = 32
GROUPS = ((0, 1, 4, 2), (3, 5, 6, 7, 8))
FULL = (1, 4)
QUARTER = (2, 3, 5, 6, 7, 8)
R2 = 512
C = 192.0 ** -0.5 * 1.4426950408889634
BIG = -1.0e30
NT = (((1,), (1,)), ((), ()))


def kernel(q_hbm, lat_ref, seg_ref, w_hbm, o_ref,
           kbuf, wbuf, qv, qs, segc, S, mx, p0, p1, l0, l1, lsum, mold, acc, ctx,
           q_sem, w_sem, sx, rx, sb, rb, ss, rs, swy, rwy, swz, rwz, sws, rws):
    dp, tp = lax.axis_index("dp"), lax.axis_index("tp")
    core = lax.rem(dp, 2)
    y = lax.rem(dp // 2, 4)
    z = dp // 8
    sib = dp + 1 - 2 * core

    def xpeer(d):
        return (dp, lax.rem(tp + d, 4))

    def ypeer(d):
        return (z * 8 + lax.rem(y + d, 4) * 2 + core, tp)

    def zpeer(d):
        return (lax.rem(z + d, 4) * 8 + y * 2 + core, tp)

    def has_dst(k):
        return dp + 2 * k <= 31

    def has_src(k):
        return dp - 2 * k >= 0

    qcopy = [pltpu.make_async_copy(q_hbm.at[:, pl.ds(g * 2 * FEAT, 2 * FEAT)], qv.at[g], q_sem.at[g]) for g in range(HEADS // 2)]
    for cp in qcopy:
        cp.start()
    wown = pltpu.make_async_copy(w_hbm, wbuf.at[:, z, y, core], w_sem.at[0])
    wown.start()

    barrier = pltpu.get_barrier_semaphore()

    def greet(dev):
        pl.semaphore_signal(barrier, inc=1, device_id=dev, device_id_type=MESH)

    for d in range(1, 4):
        greet(xpeer(d))
        greet(ypeer(d))
        greet(zpeer(d))
    greet((sib, tp))
    for k in range(1, NCH):
        @pl.when(has_src(k))
        def _():
            greet((dp - 2 * k, tp))

    seg = jnp.broadcast_to(seg_ref[...].astype(F32), (TOK, TOK))
    segc[...] = jnp.transpose(seg)
    my_rows = pl.ds(pl.multiple_of(core * TOK + tp * SHARD, SHARD), SHARD)
    half = pl.ds(pl.multiple_of(core * TOK, TOK), TOK)
    other = pl.ds(pl.multiple_of((1 - core) * TOK, TOK), TOK)
    lane32 = lax.broadcasted_iota(jnp.int32, (SHARD, 128), 1).astype(F32)
    mine = segc[pl.ds(pl.multiple_of(tp * SHARD, SHARD), SHARD), :]
    kfeat = jnp.where((lane32 >= 4.0) | (lane32 == mine), 0.0, BIG).astype(BF16)
    kbuf[0, my_rows, 0:FEAT] = lat_ref[...]
    kbuf[0, my_rows, FEAT:WIDE] = kfeat[:, :WIDE - FEAT]

    n_wait = 10 + jnp.minimum(NCH - 1, 15 - dp // 2)
    pl.semaphore_wait(barrier, n_wait)

    def xcopy(k, d):
        return pltpu.make_async_remote_copy(kbuf.at[k, my_rows, :], kbuf.at[k, my_rows, :], sx.at[k, d], rx.at[k, d], device_id=xpeer(d), device_id_type=MESH)

    def bcopy(k):
        rows = half if k in FULL else my_rows
        return pltpu.make_async_remote_copy(kbuf.at[0, rows, :], kbuf.at[k, rows, :], sb.at[k], rb.at[k], device_id=(dp + 2 * k, tp), device_id_type=MESH)

    def scopy(k):
        return pltpu.make_async_remote_copy(kbuf.at[k, half, :], kbuf.at[k, half, :], ss.at[k], rs.at[k], device_id=(sib, tp), device_id_type=MESH)

    for d in (1, 3, 2):
        xcopy(0, d).start()
    for k in QUARTER:
        @pl.when(has_dst(k))
        def _():
            bcopy(k).start()

    def wcopy(ref_src, where, ssem, rsem, dev):
        return pltpu.make_async_remote_copy(ref_src, where, ssem, rsem, device_id=dev, device_id_type=MESH)

    H2 = HEADS // 2
    lo, hi = pl.ds(0, H2), pl.ds(H2, H2)

    def wy1(d):
        return wcopy(w_hbm.at[lo], wbuf.at[lo, z, y, core], swy.at[0, d], rwy.at[0, d], ypeer(d))

    def wz1(d):
        return wcopy(w_hbm.at[hi], wbuf.at[hi, z, y, core], swz.at[0, d], rwz.at[0, d], zpeer(d))

    def wz2(d):
        return wcopy(wbuf.at[lo, z, :, core], wbuf.at[lo, z, :, core], swz.at[1, d], rwz.at[1, d], zpeer(d))

    def wy2(d):
        return wcopy(wbuf.at[hi, :, y, core], wbuf.at[hi, :, y, core], swy.at[1, d], rwy.at[1, d], ypeer(d))

    def wsib():
        return wcopy(wbuf.at[:, :, :, core], wbuf.at[:, :, :, core], sws.at[0], rws.at[0], (sib, tp))

    segv = segc[...]
    lane = lax.broadcasted_iota(jnp.int32, (TOK, 128), 1)
    onehot = jnp.where((lane - 64).astype(F32) == segv, 1.0, 0.0)

    def prep(g):
        qcopy[g].wait()
        even = qv[g, :, 0:WIDE]
        odd = pltpu.roll(qv[g, :, LATENT:2 * FEAT], WIDE - 64, 1)
        for i, v in ((0, even), (1, odd)):
            r = pl.ds((2 * g + i) * TOK, TOK)
            qs[r, 0:LATENT] = v[:, 0:LATENT]
            qs[r, LATENT:WIDE] = jnp.where(lane < 64, v[:, LATENT:WIDE].astype(F32), onehot).astype(BF16)

    for g in range(HEADS // 2):
        prep(g)

    for k in range(1, NCH):
        @pl.when(jnp.logical_not(has_src(k)))
        def _():
            ln = lax.broadcasted_iota(jnp.int32, (CHUNK, 128), 1)
            kbuf[k, :, 0:LATENT] = jnp.zeros((CHUNK, LATENT), BF16)
            kbuf[k, :, LATENT:WIDE] = jnp.where((ln >= 64) & (ln < 68), BIG, 0.0).astype(BF16)

    for d in range(1, 4):
        xcopy(0, d).wait_recv()
    scopy(0).start()
    for k in FULL:
        @pl.when(has_dst(k))
        def _():
            bcopy(k).start()
    for k in QUARTER:
        @pl.when(has_src(k))
        def _():
            bcopy(k).wait_recv()
            for d in (1, 3, 2):
                xcopy(k, d).start()
    for d in (1, 3, 2):
        wy1(d).start()
        wz1(d).start()

    def relay(k):
        @pl.when(has_src(k))
        def _():
            if k in FULL:
                bcopy(k).wait_recv()
            else:
                for d in range(1, 4):
                    xcopy(k, d).wait_recv()
            scopy(k).start()

    def arrive(k):
        if k == 0:
            scopy(0).wait_recv()
        else:
            @pl.when(has_src(k))
            def _():
                scopy(k).wait_recv()

    def score(k, slot, first):
        s = lax.dot_general(qs[...], kbuf[k], NT, preferred_element_type=F32)
        if k == 0:
            rr = lax.broadcasted_iota(jnp.int32, (ROWS, CHUNK), 0)
            cc = lax.broadcasted_iota(jnp.int32, (ROWS, CHUNK), 1)
            s = jnp.where(cc <= (rr & (TOK - 1)) + core * TOK, s, BIG)
        S[slot] = s
        m = jnp.maximum(s[:, :128], s[:, 128:])
        mx[...] = m if first else jnp.maximum(mx[...], m)

    ps, ls = (p0, p1), (l0, l1)

    def weigh(gi, r):
        rows = pl.ds(r * R2, R2)
        m = jnp.max(mx[rows, :], axis=1, keepdims=True) * C
        n = len(GROUPS[gi])
        l = None
        for j in range(n):
            p = jnp.exp2(S[j, rows, :] * C - m)
            t = p[:, :128] + p[:, 128:]
            l = t if l is None else l + t
            ps[r % 2][:, j * CHUNK:(j + 1) * CHUNK] = p.astype(BF16)
        ls[r % 2][...] = l
        return m

    def gather_values(gi):
        ks = GROUPS[gi]
        return jnp.concatenate([kbuf[k, :, 0:LATENT] for k in ks], axis=0)

    def values(gi, r, m):
        rows = pl.ds(r * R2, R2)
        n = len(GROUPS[gi])
        a = jnp.dot(ps[r % 2][:, 0:n * CHUNK], gather_values(gi), preferred_element_type=F32)
        l = ls[r % 2][...]
        last = gi == len(GROUPS) - 1
        if gi > 0:
            al = jnp.exp2(mold[rows, 0:1] - m)
            a = a + acc[rows, :] * al
            l = l + lsum[rows, :] * al
        if last:
            inv = 1.0 / jnp.sum(l, axis=1, keepdims=True)
            ctx[rows, :] = (a * inv).astype(BF16)
        else:
            acc[rows, :] = a
            lsum[rows, :] = l
            mold[rows, :] = jnp.broadcast_to(m, (R2, 128))

    order = [k for g in GROUPS for k in g]
    relay(order[1])
    pos = 0
    for gi, ks in enumerate(GROUPS):
        for slot, k in enumerate(ks):
            arrive(k)
            score(k, slot, pos == 0)
            pos += 1
            if pos + 1 < NCH:
                relay(order[pos + 1])
            if pos == 3:
                for d in range(1, 4):
                    wy1(d).wait_recv()
                    wz1(d).wait_recv()
                wown.wait()
                for d in (1, 3, 2):
                    wz2(d).start()
                    wy2(d).start()
        if gi == len(GROUPS) - 1:
            for d in range(1, 4):
                wz2(d).wait_recv()
                wy2(d).wait_recv()
            wsib().start()
        n = ROWS // R2
        m = weigh(gi, 0)
        for r in range(n):
            nm = weigh(gi, r + 1) if r + 1 < n else None
            values(gi, r, m)
            m = nm

    wsib().wait_recv()
    for h in range(HEADS):
        wv = wbuf[h].reshape(LATENT, VALUE)
        o_ref[:, h * VALUE:(h + 1) * VALUE] = jnp.dot(ctx[h * TOK:(h + 1) * TOK, :], wv, preferred_element_type=F32).astype(BF16)

    for d in range(1, 4):
        xcopy(0, d).wait_send()
        wy1(d).wait_send()
        wz1(d).wait_send()
        wy2(d).wait_send()
        wz2(d).wait_send()
    scopy(0).wait_send()
    wsib().wait_send()
    for k in range(1, NCH):
        @pl.when(has_dst(k))
        def _():
            bcopy(k).wait_send()

        @pl.when(has_src(k))
        def _():
            scopy(k).wait_send()
            if k in QUARTER:
                for d in range(1, 4):
                    xcopy(k, d).wait_send()


def per_device(queries, latents, segment_ids, value_weight):
    dma = pltpu.SemaphoreType.DMA
    gmax = max(len(g) for g in GROUPS)
    return pl.pallas_call(
        kernel,
        out_shape=jax.ShapeDtypeStruct((TOK, HEADS * VALUE), BF16),
        in_specs=[pl.BlockSpec(memory_space=pl.ANY), pl.BlockSpec(memory_space=pltpu.VMEM), pl.BlockSpec(memory_space=pltpu.VMEM), pl.BlockSpec(memory_space=pl.ANY)],
        out_specs=pl.BlockSpec(memory_space=pltpu.VMEM),
        scratch_shapes=[
            pltpu.VMEM((NCH, CHUNK, WIDE), BF16),
            pltpu.VMEM((HEADS, 4, 4, 2, 16, VALUE), BF16),
            pltpu.VMEM((HEADS // 2, TOK, 2 * FEAT), BF16),
            pltpu.VMEM((ROWS, WIDE), BF16),
            pltpu.VMEM((TOK, 128), F32),
            pltpu.VMEM((gmax, ROWS, CHUNK), F32),
            pltpu.VMEM((ROWS, 128), F32),
            pltpu.VMEM((R2, gmax * CHUNK), BF16),
            pltpu.VMEM((R2, gmax * CHUNK), BF16),
            pltpu.VMEM((R2, 128), F32),
            pltpu.VMEM((R2, 128), F32),
            pltpu.VMEM((ROWS, 128), F32),
            pltpu.VMEM((ROWS, 128), F32),
            pltpu.VMEM((ROWS, LATENT), F32),
            pltpu.VMEM((ROWS, LATENT), BF16),
            dma((HEADS // 2,)), dma((1,)),
            dma((NCH, 4)), dma((NCH, 4)),
            dma((NCH,)), dma((NCH,)),
            dma((NCH,)), dma((NCH,)),
            dma((2, 4)), dma((2, 4)),
            dma((2, 4)), dma((2, 4)),
            dma((1,)), dma((1,)),
        ],
        compiler_params=pltpu.CompilerParams(collective_id=0, has_side_effects=True, vmem_limit_bytes=56 * 2 ** 20),
        cost_estimate=pl.CostEstimate(flops=11 * 10 ** 9, bytes_accessed=8 * 10 ** 6, transcendentals=5 * 10 ** 6),
    )(queries, latents, segment_ids.reshape(1, TOK), value_weight)


def solution(mesh):
    placed = (P("dp", "tp"), P(("dp", "tp"), None), P("dp"), P("tp", "dp", None))
    return jax.shard_map(per_device, mesh=mesh, in_specs=placed, out_specs=P("dp", "tp"), check_vma=False)
```

time: 141 us -> 47.3 us (0.34); the launches traced: 138 us -> 47 us
  Pallas kernels: 0 us -> 45.2 us
  matrix products: 44.6 us -> 0 us
  blocking collectives: 36.2 us -> 0 us
  waiting for transfers between devices: 20.9 us -> 0 us
  other arithmetic: 17.1 us -> 0 us
  between operations: 13.5 us -> 0.01 us
  local copies, waits for them, and re-layouts: 5.92 us -> 1.88 us
    pallas_call x0 -> x1, Pallas kernels: none -> 45.2 us  [per_device(): pl.pallas_call(kernel, out_shape=jax.ShapeDtypeStruct((TOK, HEADS * VALUE...]
    dot_general x3 -> x0, matrix products: 44.6 us -> none  [the longest x1 23 us: per_device(): jnp.einsum('rd,kd->rk', query_rows, key_rows, preferred_element_type=jnp....]
    all_gather x2 -> x0, blocking collectives: 36.2 us -> none  [the longest x1 22.3 us: per_device(): lax.all_gather(segment_ids, 'dp', axis=0, tiled=True)[None, :]]
    all_gather x2 -> x0, waiting for transfers between devices: 20.2 us -> none  [the longest x1 20.2 us: per_device(): key_rows = lax.all_gather(local_latent, 'dp', axis=0, tiled=True)]
    reduce_sum x1 -> x0, other arithmetic: 17.1 us -> none  [per_device(): weight_sum = jnp.sum(weights, axis=1)]
    reshape x2 -> x0, local copies, waits for them, and re-layouts: 4.93 us -> none  [the longest x1 3.92 us: per_device(): query_rows = held_queries.reshape(row_count * head_count, feature_width)]
    unnamed x4 -> x1, local copies, waits for them, and re-layouts: 0.01 us -> 1.88 us
  transfers between devices with their start and end apart: 2 -> 0, of which waited for: 1 -> 0; matrix products, arithmetic and copies ran while one was open for 45% -> 0% of each run, Pallas kernels for 0% -> 0%
where the time goes in v1:
time: 47.3 us; the launch traced here: 47 us
  Pallas kernels  45.2 us (96%)
  local copies, waits for them, and re-layouts  1.88 us (4%)
    pallas_call x1, Pallas kernels, per_device(): pl.pallas_call(kernel, out_shape=jax.ShapeDtypeStruct((TOK, HEADS * VALUE...  45.2 us
    unnamed x1, local copies, waits for them, and re-layouts  1.88 us

profile of v1, /device:TPU:32, one launch (start us, length us, event | category | flops | bytes accessed | tf_op | source)
XLA Modules:
  0.0 47.0 jit_solution(4801668720652142583)
XLA Ops:
  0.0 45.2 %shard_map.46 = bf16[128,2048]{1,0:T(8,128)(2,1)} custom-call(bf16[128,9216]{1,0:T(8,128)(2,1)} %q_hbm.1, bf16[32,576]{1,0:T(8,128)(2,1)} %lat_ref.1, s32[1,128]{1,0:T(1,128)} %bitcast.1, bf16[16,16,128]{2,1,0:T(8,128)(2,1)} %w_hbm.1), custom_call_target="tpu_custom_call" | custom-call | flops 11000000512 | bytes 8000000 | tf_op jit(solution)/shard_map/pallas_call | solution.py:291
  45.2 1.9 %copy.6 = bf16[128,2048]{1,0:T(8,128)(2,1)} copy(bf16[128,2048]{1,0:T(8,128)(2,1)} %shard_map.46) | data formatting | bytes 1048576

commit v2 on v1

--- a/solution.py
+++ b/solution.py
@@ -18,9 +18,11 @@
 CHUNK = 2 * TOK
 NCH = 9
 SHARD = 32
-GROUPS = ((0, 1, 4, 2), (3, 5, 6, 7, 8))
-FULL = (1, 4)
-QUARTER = (2, 3, 5, 6, 7, 8)
+GROUPS = ((0, 4, 1, 3), (8, 2, 6, 5, 7))
+DIRECT = (1, 3)
+ALONG = (5, 7)
+SHARDS = (1, 3, 2, 6, 5, 7)
+R1 = 512
 R2 = 512
 C = 192.0 ** -0.5 * 1.4426950408889634
 BIG = -1.0e30
@@ -29,7 +31,7 @@
 
 def kernel(q_hbm, lat_ref, seg_ref, w_hbm, o_ref,
            kbuf, wbuf, qv, qs, segc, S, mx, p0, p1, l0, l1, lsum, mold, acc, ctx,
-           q_sem, w_sem, sx, rx, sb, rb, ss, rs, swy, rwy, swz, rwz, sws, rws):
+           q_sem, w_sem, sx, rx, sb, sy, ry, sz, rz, ss, rs, swy, rwy, swz, rwz, sws, rws):
     dp, tp = lax.axis_index("dp"), lax.axis_index("tp")
     core = lax.rem(dp, 2)
     y = lax.rem(dp // 2, 4)
@@ -45,9 +47,6 @@
     def zpeer(d):
         return (lax.rem(z + d, 4) * 8 + y * 2 + core, tp)
 
-    def has_dst(k):
-        return dp + 2 * k <= 31
-
     def has_src(k):
         return dp - 2 * k >= 0
 
@@ -67,8 +66,8 @@
         greet(ypeer(d))
         greet(zpeer(d))
     greet((sib, tp))
-    for k in range(1, NCH):
-        @pl.when(has_src(k))
+    for k in DIRECT:
+        @pl.when((core == 0) & has_src(k))
         def _():
             greet((dp - 2 * k, tp))
 
@@ -83,46 +82,76 @@
     kbuf[0, my_rows, 0:FEAT] = lat_ref[...]
     kbuf[0, my_rows, FEAT:WIDE] = kfeat[:, :WIDE - FEAT]
 
-    n_wait = 10 + jnp.minimum(NCH - 1, 15 - dp // 2)
+    n_wait = 10 + jnp.where(core == 0, jnp.where(dp + 2 <= 31, 1, 0) + jnp.where(dp + 6 <= 31, 1, 0), 0)
     pl.semaphore_wait(barrier, n_wait)
 
+    def remote(ref, dst, ssem, rsem, dev):
+        return pltpu.make_async_remote_copy(ref, dst, ssem, rsem, device_id=dev, device_id_type=MESH)
+
+    def zdev(v):
+        return (v * 8 + y * 2 + core, tp)
+
     def xcopy(k, d):
-        return pltpu.make_async_remote_copy(kbuf.at[k, my_rows, :], kbuf.at[k, my_rows, :], sx.at[k, d], rx.at[k, d], device_id=xpeer(d), device_id_type=MESH)
+        at = kbuf.at[k, my_rows, :]
+        return remote(at, at, sx.at[k, d], rx.at[k, d], xpeer(d))
+
+    def zcopy(r):
+        return remote(kbuf.at[0, my_rows, :], kbuf.at[4 * r, my_rows, :], sz.at[r], rz.at[r], zdev(lax.rem(z + r, 4)))
+
+    first = core == 0
+    second = core == 1
+
+    def yrow(k):
+        return k // 4 + jnp.where(y + k % 4 <= 3, 0, 1)
+
+    def ycopy(k, rows):
+        return remote(kbuf.at[4 * yrow(k), rows, :], kbuf.at[k, rows, :], sy.at[k], ry.at[k], ypeer(k % 4))
+
+    def yneed(k):
+        return z >= yrow(k)
 
     def bcopy(k):
-        rows = half if k in FULL else my_rows
-        return pltpu.make_async_remote_copy(kbuf.at[0, rows, :], kbuf.at[k, rows, :], sb.at[k], rb.at[k], device_id=(dp + 2 * k, tp), device_id_type=MESH)
+        return remote(kbuf.at[0, half, :], kbuf.at[k, half, :], sb.at[k], ry.at[k], (dp + 2 * k, tp))
 
     def scopy(k):
-        return pltpu.make_async_remote_copy(kbuf.at[k, half, :], kbuf.at[k, half, :], ss.at[k], rs.at[k], device_id=(sib, tp), device_id_type=MESH)
-
+        at = kbuf.at[k, half, :]
+        return remote(at, at, ss.at[k], rs.at[k], (sib, tp))
+
+    H2 = HEADS // 2
+
+    lo, hi = pl.ds(0, H2), pl.ds(H2, H2)
+
+    def wy1(d):
+        return remote(w_hbm.at[lo], wbuf.at[lo, z, y, core], swy.at[0, d], rwy.at[0, d], ypeer(d))
+
+    def wz1(d):
+        return remote(w_hbm.at[hi], wbuf.at[hi, z, y, core], swz.at[0, d], rwz.at[0, d], zpeer(d))
+
+    def wz2(d):
+        at = wbuf.at[lo, z, :, core]
+        return remote(at, at, swz.at[1, d], rwz.at[1, d], zpeer(d))
+
+    def wy2(d):
+        at = wbuf.at[hi, :, y, core]
+        return remote(at, at, swy.at[1, d], rwy.at[1, d], ypeer(d))
+
+    def wsib(i):
+        at = wbuf.at[(lo, hi)[i], :, :, core]
+        return remote(at, at, sws.at[i], rws.at[i], (sib, tp))
+
+    def shards(k):
+        return second if k in DIRECT + ALONG else True
+
+    for r in (1, 2):
+        @pl.when(z + r <= 3)
+        def _():
+            zcopy(r).start()
     for d in (1, 3, 2):
         xcopy(0, d).start()
-    for k in QUARTER:
-        @pl.when(has_dst(k))
-        def _():
-            bcopy(k).start()
-
-    def wcopy(ref_src, where, ssem, rsem, dev):
-        return pltpu.make_async_remote_copy(ref_src, where, ssem, rsem, device_id=dev, device_id_type=MESH)
-
-    H2 = HEADS // 2
-    lo, hi = pl.ds(0, H2), pl.ds(H2, H2)
-
-    def wy1(d):
-        return wcopy(w_hbm.at[lo], wbuf.at[lo, z, y, core], swy.at[0, d], rwy.at[0, d], ypeer(d))
-
-    def wz1(d):
-        return wcopy(w_hbm.at[hi], wbuf.at[hi, z, y, core], swz.at[0, d], rwz.at[0, d], zpeer(d))
-
-    def wz2(d):
-        return wcopy(wbuf.at[lo, z, :, core], wbuf.at[lo, z, :, core], swz.at[1, d], rwz.at[1, d], zpeer(d))
-
-    def wy2(d):
-        return wcopy(wbuf.at[hi, :, y, core], wbuf.at[hi, :, y, core], swy.at[1, d], rwy.at[1, d], ypeer(d))
-
-    def wsib():
-        return wcopy(wbuf.at[:, :, :, core], wbuf.at[:, :, :, core], sws.at[0], rws.at[0], (sib, tp))
+    for k in SHARDS:
+        @pl.when((yrow(k) == 0) & shards(k))
+        def _():
+            ycopy(k, my_rows).start()
 
     segv = segc[...]
     lane = lax.broadcasted_iota(jnp.int32, (TOK, 128), 1)
@@ -137,9 +166,6 @@
             qs[r, 0:LATENT] = v[:, 0:LATENT]
             qs[r, LATENT:WIDE] = jnp.where(lane < 64, v[:, LATENT:WIDE].astype(F32), onehot).astype(BF16)
 
-    for g in range(HEADS // 2):
-        prep(g)
-
     for k in range(1, NCH):
         @pl.when(jnp.logical_not(has_src(k)))
         def _():
@@ -147,31 +173,75 @@
             kbuf[k, :, 0:LATENT] = jnp.zeros((CHUNK, LATENT), BF16)
             kbuf[k, :, LATENT:WIDE] = jnp.where((ln >= 64) & (ln < 68), BIG, 0.0).astype(BF16)
 
+    for g in range(HEADS // 2):
+        prep(g)
+
+    for r in (1, 2):
+        @pl.when(z >= r)
+        def _():
+            zcopy(r).wait_recv()
+            if r == 1:
+                for d in (1, 3, 2):
+                    xcopy(4, d).start()
+        for k in SHARDS:
+            @pl.when(yneed(k) & (yrow(k) == r) & shards(k))
+            def _():
+                ycopy(k, my_rows).start()
     for d in range(1, 4):
         xcopy(0, d).wait_recv()
     scopy(0).start()
-    for k in FULL:
-        @pl.when(has_dst(k))
+    for k in DIRECT:
+        @pl.when(first & (dp + 2 * k <= 31))
         def _():
             bcopy(k).start()
-    for k in QUARTER:
-        @pl.when(has_src(k))
-        def _():
-            bcopy(k).wait_recv()
+    for d in (1, 3, 2):
+        wz1(d).start()
+        wy1(d).start()
+
+    def issue(k):
+        @pl.when(shards(k) & has_src(k))
+        def _():
+            ycopy(k, my_rows).wait_recv()
             for d in (1, 3, 2):
                 xcopy(k, d).start()
-    for d in (1, 3, 2):
-        wy1(d).start()
-        wz1(d).start()
+
+    def along(k):
+        @pl.when(first & yneed(k))
+        def _():
+            ycopy(k, half).start()
+
+    def weights2():
+        wown.wait()
+        for d in range(1, 4):
+            wy1(d).wait_recv()
+        for d in (1, 3, 2):
+            wz2(d).start()
+        for d in range(1, 4):
+            wz1(d).wait_recv()
+        for d in (1, 3, 2):
+            wy2(d).start()
+
+    def weights4():
+        for d in range(1, 4):
+            wz2(d).wait_recv()
+        wsib(0).start()
+
+    def weights5():
+        for d in range(1, 4):
+            wy2(d).wait_recv()
+        wsib(1).start()
 
     def relay(k):
-        @pl.when(has_src(k))
-        def _():
-            if k in FULL:
-                bcopy(k).wait_recv()
-            else:
-                for d in range(1, 4):
-                    xcopy(k, d).wait_recv()
+        if k in DIRECT + ALONG:
+            @pl.when(first & has_src(k))
+            def _():
+                (bcopy(k) if k in DIRECT else ycopy(k, half)).wait_recv()
+                scopy(k).start()
+
+        @pl.when(has_src(k) & shards(k))
+        def _():
+            for d in range(1, 4):
+                xcopy(k, d).wait_recv()
             scopy(k).start()
 
     def arrive(k):
@@ -183,14 +253,16 @@
                 scopy(k).wait_recv()
 
     def score(k, slot, first):
-        s = lax.dot_general(qs[...], kbuf[k], NT, preferred_element_type=F32)
-        if k == 0:
-            rr = lax.broadcasted_iota(jnp.int32, (ROWS, CHUNK), 0)
-            cc = lax.broadcasted_iota(jnp.int32, (ROWS, CHUNK), 1)
-            s = jnp.where(cc <= (rr & (TOK - 1)) + core * TOK, s, BIG)
-        S[slot] = s
-        m = jnp.maximum(s[:, :128], s[:, 128:])
-        mx[...] = m if first else jnp.maximum(mx[...], m)
+        for r in range(ROWS // R1):
+            rows = pl.ds(r * R1, R1)
+            s = lax.dot_general(qs[rows, :], kbuf[k], NT, preferred_element_type=F32)
+            if k == 0:
+                rr = lax.broadcasted_iota(jnp.int32, (R1, CHUNK), 0)
+                cc = lax.broadcasted_iota(jnp.int32, (R1, CHUNK), 1)
+                s = jnp.where(cc <= (rr & (TOK - 1)) + core * TOK, s, BIG)
+            S[slot, rows, :] = s
+            m = jnp.maximum(s[:, :128], s[:, 128:])
+            mx[rows, :] = m if first else jnp.maximum(mx[rows, :], m)
 
     ps, ls = (p0, p1), (l0, l1)
 
@@ -229,38 +301,64 @@
             lsum[rows, :] = l
             mold[rows, :] = jnp.broadcast_to(m, (R2, 128))
 
-    order = [k for g in GROUPS for k in g]
-    relay(order[1])
-    pos = 0
-    for gi, ks in enumerate(GROUPS):
-        for slot, k in enumerate(ks):
-            arrive(k)
-            score(k, slot, pos == 0)
-            pos += 1
-            if pos + 1 < NCH:
-                relay(order[pos + 1])
-            if pos == 3:
-                for d in range(1, 4):
-                    wy1(d).wait_recv()
-                    wz1(d).wait_recv()
-                wown.wait()
-                for d in (1, 3, 2):
-                    wz2(d).start()
-                    wy2(d).start()
-        if gi == len(GROUPS) - 1:
-            for d in range(1, 4):
-                wz2(d).wait_recv()
-                wy2(d).wait_recv()
-            wsib().start()
+    def finish(gi, between=()):
         n = ROWS // R2
         m = weigh(gi, 0)
         for r in range(n):
             nm = weigh(gi, r + 1) if r + 1 < n else None
             values(gi, r, m)
             m = nm
-
-    wsib().wait_recv()
+            if r < len(between) and between[r] is not None:
+                between[r]()
+
+    def ring8():
+        @pl.when(z >= 2)
+        def _():
+            for d in (1, 3, 2):
+                xcopy(8, d).start()
+
+    arrive(0)
+    score(0, 0, True)
+    issue(1)
+    issue(3)
+    ring8()
+    relay(4)
+    issue(2)
+    arrive(4)
+    score(4, 1, False)
+    relay(1)
+    issue(6)
+    issue(5)
+    issue(7)
+    weights2()
+    arrive(1)
+    score(1, 2, False)
+    relay(3)
+    relay(8)
+    along(5)
+    along(7)
+    arrive(3)
+    score(3, 3, False)
+    finish(0, [None, lambda: relay(2)])
+    arrive(8)
+    score(8, 0, False)
+    relay(6)
+    arrive(2)
+    score(2, 1, False)
+    relay(5)
+    arrive(6)
+    score(6, 2, False)
+    relay(7)
+    arrive(5)
+    score(5, 3, False)
+    arrive(7)
+    score(7, 4, False)
+    weights4()
+    finish(1, [None, weights5])
+
     for h in range(HEADS):
+        if h % H2 == 0:
+            wsib(h // H2).wait_recv()
         wv = wbuf[h].reshape(LATENT, VALUE)
         o_ref[:, h * VALUE:(h + 1) * VALUE] = jnp.dot(ctx[h * TOK:(h + 1) * TOK, :], wv, preferred_element_type=F32).astype(BF16)
 
@@ -270,19 +368,36 @@
         wz1(d).wait_send()
         wy2(d).wait_send()
         wz2(d).wait_send()
+    wsib(0).wait_send()
+    wsib(1).wait_send()
+    for r in (1, 2):
+        @pl.when(z + r <= 3)
+        def _():
+            zcopy(r).wait_send()
+
+    for k in SHARDS:
+        @pl.when(yneed(k) & shards(k))
+        def _():
+            ycopy(k, my_rows).wait_send()
+    for k in DIRECT:
+        @pl.when(first & (dp + 2 * k <= 31))
+        def _():
+            bcopy(k).wait_send()
+    for k in ALONG:
+        @pl.when(first & yneed(k))
+        def _():
+            ycopy(k, half).wait_send()
+
     scopy(0).wait_send()
-    wsib().wait_send()
     for k in range(1, NCH):
-        @pl.when(has_dst(k))
-        def _():
-            bcopy(k).wait_send()
-
         @pl.when(has_src(k))
         def _():
             scopy(k).wait_send()
-            if k in QUARTER:
-                for d in range(1, 4):
-                    xcopy(k, d).wait_send()
+
+        @pl.when(has_src(k) & shards(k))
+        def _():
+            for d in range(1, 4):
+                xcopy(k, d).wait_send()
 
 
 def per_device(queries, latents, segment_ids, value_weight):
@@ -311,11 +426,12 @@
             pltpu.VMEM((ROWS, LATENT), BF16),
             dma((HEADS // 2,)), dma((1,)),
             dma((NCH, 4)), dma((NCH, 4)),
-            dma((NCH,)), dma((NCH,)),
+            dma((NCH,)), dma((NCH,)), dma((NCH,)),
+            dma((3,)), dma((3,)),
             dma((NCH,)), dma((NCH,)),
             dma((2, 4)), dma((2, 4)),
             dma((2, 4)), dma((2, 4)),
-            dma((1,)), dma((1,)),
+            dma((2,)), dma((2,)),
         ],
         compiler_params=pltpu.CompilerParams(collective_id=0, has_side_effects=True, vmem_limit_bytes=56 * 2 ** 20),
         cost_estimate=pl.CostEstimate(flops=11 * 10 ** 9, bytes_accessed=8 * 10 ** 6, transcendentals=5 * 10 ** 6),

time: 47.3 us -> 40.1 us (0.85)
  the two profiles are of different devices: /device:TPU:32 before, /device:TPU:65 now
where the time goes in v2:
time: 40.1 us; the launch traced here: 39.9 us
  Pallas kernels  38 us (95%)
  local copies, waits for them, and re-layouts  1.88 us (5%)
    pallas_call x1, Pallas kernels, per_device(): pl.pallas_call(kernel, out_shape=jax.ShapeDtypeStruct((TOK, HEADS * VALUE...  38 us
    unnamed x1, local copies, waits for them, and re-layouts  1.88 us

profile of v2, /device:TPU:65, one launch (start us, length us, event | category | flops | bytes accessed | tf_op | source)
XLA Modules:
  0.0 39.9 jit_solution(9085776464677806863)
XLA Ops:
  0.0 38.0 %shard_map.46 = bf16[128,2048]{1,0:T(8,128)(2,1)} custom-call(bf16[128,9216]{1,0:T(8,128)(2,1)} %q_hbm.1, bf16[32,576]{1,0:T(8,128)(2,1)} %lat_ref.1, s32[1,128]{1,0:T(1,128)} %bitcast.1, bf16[16,16,128]{2,1,0:T(8,128)(2,1)} %w_hbm.1), custom_call_target="tpu_custom_call" | custom-call | flops 11000000512 | bytes 8000000 | tf_op jit(solution)/shard_map/pallas_call | solution.py:406
  38.0 1.9 %copy.6 = bf16[128,2048]{1,0:T(8,128)(2,1)} copy(bf16[128,2048]{1,0:T(8,128)(2,1)} %shard_map.46) | data formatting | bytes 1048576

commit v3 on v2

v3 whole, which is shorter than its diff:
```python
import functools

import jax
import jax.numpy as jnp
from jax import lax
from jax.experimental import pallas as pl
from jax.experimental.pallas import tpu as pltpu
from jax.sharding import PartitionSpec as P

MESH = pl.DeviceIdType.MESH
F32, BF16 = jnp.float32, jnp.bfloat16
LATENT, ROPE, VALUE = 512, 64, 128
FEAT = LATENT + ROPE
WIDE = 640
TOK = 128
HEADS = 16
ROWS = TOK * HEADS
CHUNK = 2 * TOK
NCH = 9
SHARD = 32
DIRECT = (1, 3)
ALONG = (5, 7)
SHARDS = (1, 3, 2, 6, 5, 7)
RB = 512
STEPS = ((0,), (4, 8), (1, 3), (2, 6), (5, 7))
C = 192.0 ** -0.5 * 1.4426950408889634
BIG = -1.0e30
NT = (((1,), (1,)), ((), ()))


def kernel(q_hbm, lat_hbm, seg_hbm, w_hbm, o_ref,
           lat_ref, seg_ref, in_sem, kbuf, wbuf, qv, qs, segc, S, mx, lsum, top, acc, ctx,
           q_sem, w_sem, sx, rx, sb, sy, ry, sz, rz, ss, rs, swy, rwy, swz, rwz, sws, rws):
    dp, tp = lax.axis_index("dp"), lax.axis_index("tp")
    core = lax.rem(dp, 2)
    y = lax.rem(dp // 2, 4)
    z = dp // 8
    sib = dp + 1 - 2 * core

    def xpeer(d):
        return (dp, lax.rem(tp + d, 4))

    def ypeer(d):
        return (z * 8 + lax.rem(y + d, 4) * 2 + core, tp)

    def zpeer(d):
        return (lax.rem(z + d, 4) * 8 + y * 2 + core, tp)

    def has_src(k):
        return dp - 2 * k >= 0

    icopy = [pltpu.make_async_copy(lat_hbm, lat_ref, in_sem.at[0]), pltpu.make_async_copy(seg_hbm, seg_ref, in_sem.at[1])]
    for cp in icopy:
        cp.start()
    qcopy = [pltpu.make_async_copy(q_hbm.at[:, pl.ds(g * 2 * FEAT, 2 * FEAT)], qv.at[g], q_sem.at[g]) for g in range(HEADS // 2)]
    for cp in qcopy:
        cp.start()
    wown = pltpu.make_async_copy(w_hbm, wbuf.at[:, z, y, core], w_sem.at[0])
    wown.start()

    barrier = pltpu.get_barrier_semaphore()

    def greet(dev):
        pl.semaphore_signal(barrier, inc=1, device_id=dev, device_id_type=MESH)

    for d in range(1, 4):
        greet(xpeer(d))
        greet(ypeer(d))
        greet(zpeer(d))
    greet((sib, tp))
    for k in DIRECT:
        @pl.when((core == 0) & has_src(k))
        def _():
            greet((dp - 2 * k, tp))

    for cp in icopy:
        cp.wait()
    seg = jnp.broadcast_to(seg_ref[...].astype(F32), (TOK, TOK))
    segc[...] = jnp.transpose(seg)
    my_rows = pl.ds(pl.multiple_of(core * TOK + tp * SHARD, SHARD), SHARD)
    half = pl.ds(pl.multiple_of(core * TOK, TOK), TOK)
    other = pl.ds(pl.multiple_of((1 - core) * TOK, TOK), TOK)
    lane32 = lax.broadcasted_iota(jnp.int32, (SHARD, 128), 1).astype(F32)
    mine = segc[pl.ds(pl.multiple_of(tp * SHARD, SHARD), SHARD), :]
    kfeat = jnp.where((lane32 >= 4.0) | (lane32 == mine), 0.0, BIG).astype(BF16)
    kbuf[0, my_rows, 0:FEAT] = lat_ref[...]
    kbuf[0, my_rows, FEAT:WIDE] = kfeat[:, :WIDE - FEAT]

    n_wait = 10 + jnp.where(core == 0, jnp.where(dp + 2 <= 31, 1, 0) + jnp.where(dp + 6 <= 31, 1, 0), 0)
    pl.semaphore_wait(barrier, n_wait)

    def remote(ref, dst, ssem, rsem, dev):
        return pltpu.make_async_remote_copy(ref, dst, ssem, rsem, device_id=dev, device_id_type=MESH)

    def zdev(v):
        return (v * 8 + y * 2 + core, tp)

    def xcopy(k, d):
        at = kbuf.at[k, my_rows, :]
        return remote(at, at, sx.at[k], rx.at[k], xpeer(d))

    def xthree(k):
        at = kbuf.at[k, pl.ds(0, 3 * SHARD), :]
        return remote(at, at, sx.at[k], rx.at[k], xpeer(1))

    def zcopy(r):
        return remote(kbuf.at[0, my_rows, :], kbuf.at[4 * r, my_rows, :], sz.at[r], rz.at[r], zdev(lax.rem(z + r, 4)))

    first = core == 0
    second = core == 1

    def yrow(k):
        return k // 4 + jnp.where(y + k % 4 <= 3, 0, 1)

    def ycopy(k, rows):
        return remote(kbuf.at[4 * yrow(k), rows, :], kbuf.at[k, rows, :], sy.at[k], ry.at[k], ypeer(k % 4))

    def yneed(k):
        return z >= yrow(k)

    def bcopy(k):
        return remote(kbuf.at[0, half, :], kbuf.at[k, half, :], sb.at[k], ry.at[k], (dp + 2 * k, tp))

    def scopy(k):
        at = kbuf.at[k, half, :]
        return remote(at, at, ss.at[k], rs.at[k], (sib, tp))

    H2 = HEADS // 2

    lo, hi = pl.ds(0, H2), pl.ds(H2, H2)

    def wy1(d):
        return remote(w_hbm.at[lo], wbuf.at[lo, z, y, core], swy.at[0], rwy.at[0], ypeer(d))

    def wz1(d):
        return remote(w_hbm.at[hi], wbuf.at[hi, z, y, core], swz.at[0], rwz.at[0], zpeer(d))

    def wz2(d):
        at = wbuf.at[lo, z, :, core]
        return remote(at, at, swz.at[1], rwz.at[1], zpeer(d))

    def wy2(d):
        at = wbuf.at[hi, :, y, core]
        return remote(at, at, swy.at[1], rwy.at[1], ypeer(d))

    def wthree(along_y, stage):
        at = wbuf.at[lo, pl.ds(0, 3), 0, 0] if stage == 0 else wbuf.at[lo, pl.ds(0, 3), :, 0]
        if along_y:
            return remote(at, at, swy.at[stage], rwy.at[stage], ypeer(1))
        return remote(at, at, swz.at[stage], rwz.at[stage], zpeer(1))

    def wsib(i):
        at = wbuf.at[(lo, hi)[i], :, :, core]
        return remote(at, at, sws.at[i], rws.at[i], (sib, tp))

    def shards(k):
        return second if k in DIRECT + ALONG else True

    for r in (1, 2):
        @pl.when(z + r <= 3)
        def _():
            zcopy(r).start()
    for d in (1, 3, 2):
        xcopy(0, d).start()
    for k in SHARDS:
        @pl.when((yrow(k) == 0) & shards(k))
        def _():
            ycopy(k, my_rows).start()

    segv = segc[...]
    lane = lax.broadcasted_iota(jnp.int32, (TOK, 128), 1)
    onehot = jnp.where((lane - 64).astype(F32) == segv, 1.0, 0.0)

    def prep(g):
        qcopy[g].wait()
        even = qv[g, :, 0:WIDE]
        odd = pltpu.roll(qv[g, :, LATENT:2 * FEAT], WIDE - 64, 1)
        for i, v in ((0, even), (1, odd)):
            r = pl.ds((2 * g + i) * TOK, TOK)
            qs[r, 0:LATENT] = v[:, 0:LATENT]
            qs[r, LATENT:WIDE] = jnp.where(lane < 64, v[:, LATENT:WIDE].astype(F32), onehot).astype(BF16)

    for k in range(1, NCH):
        @pl.when(jnp.logical_not(has_src(k)))
        def _():
            ln = lax.broadcasted_iota(jnp.int32, (CHUNK, 128), 1)
            kbuf[k, :, 0:LATENT] = jnp.zeros((CHUNK, LATENT), BF16)
            kbuf[k, :, LATENT:WIDE] = jnp.where((ln >= 64) & (ln < 68), BIG, 0.0).astype(BF16)

    for g in range(HEADS // 2):
        prep(g)

    for r in (1, 2):
        @pl.when(z >= r)
        def _():
            zcopy(r).wait_recv()
            for d in (1, 3, 2):
                xcopy(4 * r, d).start()
        for k in SHARDS:
            @pl.when(yneed(k) & (yrow(k) == r) & shards(k))
            def _():
                ycopy(k, my_rows).start()
    for d in (1, 3, 2):
        wz1(d).start()
        wy1(d).start()
    xthree(0).wait_recv()
    scopy(0).start()
    for k in DIRECT:
        @pl.when(first & (dp + 2 * k <= 31))
        def _():
            bcopy(k).start()
    def issue(k):
        @pl.when(shards(k) & has_src(k))
        def _():
            ycopy(k, my_rows).wait_recv()
            for d in (1, 3, 2):
                xcopy(k, d).start()

    def along(k, r):
        @pl.when(first & yneed(k) & (yrow(k) == r))
        def _():
            ycopy(k, half).start()

    def weights2():
        wown.wait()
        wthree(True, 0).wait_recv()
        for d in (1, 3, 2):
            wz2(d).start()
        wthree(False, 0).wait_recv()
        for d in (1, 3, 2):
            wy2(d).start()

    def weights4():
        wthree(False, 1).wait_recv()
        wsib(0).start()

    def weights5():
        wthree(True, 1).wait_recv()
        wsib(1).start()

    def relay(k, who=None):
        if k in DIRECT + ALONG:
            @pl.when(first & has_src(k))
            def _():
                (bcopy(k) if k in DIRECT else ycopy(k, half)).wait_recv()
                scopy(k).start()

        mine = shards(k) if who is None else who

        @pl.when(has_src(k) & mine)
        def _():
            xthree(k).wait_recv()
            scopy(k).start()

    def arrive(k):
        if k == 0:
            scopy(0).wait_recv()
        else:
            @pl.when(has_src(k))
            def _():
                scopy(k).wait_recv()

    def score(ks, slot, r):
        rows = pl.ds(r * RB, RB)
        best = None
        for j, k in enumerate(ks):
            s = lax.dot_general(qs[rows, :], kbuf[k], NT, preferred_element_type=F32)
            if k == 0:
                rr = lax.broadcasted_iota(jnp.int32, (RB, CHUNK), 0)
                cc = lax.broadcasted_iota(jnp.int32, (RB, CHUNK), 1)
                s = jnp.where(cc <= (rr & (TOK - 1)) + core * TOK, s, BIG)
            S[slot, j, rows, :] = s
            m = jnp.maximum(s[:, :128], s[:, 128:])
            best = m if best is None else jnp.maximum(best, m)
        mx[slot, rows, :] = best

    def values(ks, slot, r, begin, last):
        rows = pl.ds(r * RB, RB)
        m = jnp.max(mx[slot, rows, :], axis=1, keepdims=True) * C
        if not begin:
            m = jnp.maximum(m, top[rows, 0:1])
        l, ps = None, []
        for j in range(len(ks)):
            p = jnp.exp2(S[slot, j, rows, :] * C - m)
            t = p[:, :128] + p[:, 128:]
            l = t if l is None else l + t
            ps.append(p.astype(BF16))
        p = jnp.concatenate(ps, axis=1) if len(ks) > 1 else ps[0]
        v = jnp.concatenate([kbuf[k, :, 0:LATENT] for k in ks], axis=0)
        a = jnp.dot(p, v, preferred_element_type=F32)
        if not begin:
            al = jnp.exp2(top[rows, 0:1] - m)
            a = a + acc[rows, :] * al
            l = l + lsum[rows, :] * al
        if last:
            inv = 1.0 / jnp.sum(l, axis=1, keepdims=True)
            ctx[rows, :] = (a * inv).astype(BF16)
        else:
            acc[rows, :] = a
            lsum[rows, :] = l
            top[rows, :] = jnp.broadcast_to(m, (RB, 128))

    def step(i):
        for r in range(ROWS // RB):
            if i < len(STEPS):
                score(STEPS[i], i % 2, r)
            if i > 0:
                values(STEPS[i - 1], (i - 1) % 2, r, i == 1, i == len(STEPS))

    issue(1)
    issue(3)
    arrive(0)
    step(0)
    issue(2)
    issue(6)
    issue(5)
    issue(7)
    relay(4)
    along(5, 1)
    along(7, 1)
    relay(8)
    along(5, 2)
    along(7, 2)
    weights2()
    arrive(4)
    arrive(8)
    step(1)
    relay(1)
    relay(3)
    arrive(1)
    arrive(3)
    step(2)
    relay(2)
    relay(6)
    relay(5)
    relay(7)
    arrive(2)
    arrive(6)
    step(3)
    arrive(5)
    arrive(7)
    weights4()
    step(4)
    weights5()
    step(5)

    for h in range(HEADS):
        if h % H2 == 0:
            wsib(h // H2).wait_recv()
        wv = wbuf[h].reshape(LATENT, VALUE)
        o_ref[:, h * VALUE:(h + 1) * VALUE] = jnp.dot(ctx[h * TOK:(h + 1) * TOK, :], wv, preferred_element_type=F32).astype(BF16)

    xthree(0).wait_send()
    for stage in range(2):
        wthree(True, stage).wait_send()
        wthree(False, stage).wait_send()
        wsib(stage).wait_send()
    for r in (1, 2):
        @pl.when(z + r <= 3)
        def _():
            zcopy(r).wait_send()

    for k in SHARDS:
        @pl.when(yneed(k) & shards(k))
        def _():
            ycopy(k, my_rows).wait_send()
    for k in DIRECT:
        @pl.when(first & (dp + 2 * k <= 31))
        def _():
            bcopy(k).wait_send()
    for k in ALONG:
        @pl.when(first & yneed(k))
        def _():
            ycopy(k, half).wait_send()

    scopy(0).wait_send()
    for k in range(1, NCH):
        @pl.when(has_src(k))
        def _():
            scopy(k).wait_send()

        @pl.when(has_src(k) & shards(k))
        def _():
            xthree(k).wait_send()


def per_device(queries, latents, segment_ids, value_weight):
    dma = pltpu.SemaphoreType.DMA
    return pl.pallas_call(
        kernel,
        out_shape=pltpu.VMEM((TOK, HEADS * VALUE), BF16),
        in_specs=[pl.BlockSpec(memory_space=pltpu.HBM)] * 4,
        out_specs=pl.BlockSpec(memory_space=pltpu.VMEM),
        scratch_shapes=[
            pltpu.VMEM((SHARD, FEAT), BF16), pltpu.VMEM((1, TOK), jnp.int32), dma((2,)),
            pltpu.VMEM((NCH, CHUNK, WIDE), BF16),
            pltpu.VMEM((HEADS, 4, 4, 2, 16, VALUE), BF16),
            pltpu.VMEM((HEADS // 2, TOK, 2 * FEAT), BF16),
            pltpu.VMEM((ROWS, WIDE), BF16),
            pltpu.VMEM((TOK, 128), F32),
            pltpu.VMEM((2, max(len(g) for g in STEPS), ROWS, CHUNK), F32),
            pltpu.VMEM((2, ROWS, 128), F32),
            pltpu.VMEM((ROWS, 128), F32),
            pltpu.VMEM((ROWS, 128), F32),
            pltpu.VMEM((ROWS, LATENT), F32),
            pltpu.VMEM((ROWS, LATENT), BF16),
            dma((HEADS // 2,)), dma((1,)),
            dma((NCH,)), dma((NCH,)),
            dma((NCH,)), dma((NCH,)), dma((NCH,)),
            dma((3,)), dma((3,)),
            dma((NCH,)), dma((NCH,)),
            dma((2,)), dma((2,)),
            dma((2,)), dma((2,)),
            dma((2,)), dma((2,)),
        ],
        compiler_params=pltpu.CompilerParams(collective_id=0, has_side_effects=True, vmem_limit_bytes=48 * 2 ** 20),
        cost_estimate=pl.CostEstimate(flops=11 * 10 ** 9, bytes_accessed=8 * 10 ** 6, transcendentals=5 * 10 ** 6),
    )(*[pltpu.with_memory_space_constraint(x, pltpu.HBM) for x in (queries, latents, segment_ids.reshape(1, TOK), value_weight)])


def solution(mesh):
    placed = (P("dp", "tp"), P(("dp", "tp"), None), P("dp"), P("tp", "dp", None))
    return jax.shard_map(per_device, mesh=mesh, in_specs=placed, out_specs=P("dp", "tp"), check_vma=False)
```

time: 40.1 us -> 35.5 us (0.89)
  the two profiles are of different devices: /device:TPU:65 before, /device:TPU:89 now
where the time goes in v3:
time: 35.5 us; the launch traced here: 35.3 us
  Pallas kernels  34.5 us (97%)
  local copies, waits for them, and re-layouts  0.8 us (2%)
    pallas_call x1, Pallas kernels, per_device(): pl.pallas_call(kernel, out_shape=pltpu.VMEM((TOK, HEADS * VALUE), BF16),...  34.5 us
    unnamed x1, local copies, waits for them, and re-layouts  0.8 us

profile of v3, /device:TPU:89, one launch (start us, length us, event | category | flops | bytes accessed | tf_op | source)
XLA Modules:
  0.0 35.3 jit_solution(5331286328155416490)
XLA Ops:
  0.0 34.5 %shard_map.46 = bf16[128,2048]{1,0:T(8,128)(2,1)S(1)} custom-call(bf16[128,9216]{1,0:T(8,128)(2,1)} %q_hbm.1, bf16[32,576]{1,0:T(8,128)(2,1)} %lat_hbm.1, s32[1,128]{1,0:T(1,128)} %bitcast.1, bf16[16,16,128]{2,1,0:T(8,128)(2,1)} %w_hbm.1), custom_call_target="tpu_custom_call" | custom-call | flops 11000000512 | bytes 8000000 | tf_op jit(solution)/shard_map/pallas_call | solution.py:389
  34.5 0.8 %copy.6 = bf16[128,2048]{1,0:T(8,128)(2,1)} copy(bf16[128,2048]{1,0:T(8,128)(2,1)S(1)} %shard_map.46) | data formatting | bytes 1048576

commit v4 on v3

--- a/solution.py
+++ b/solution.py
@@ -21,8 +21,9 @@
 DIRECT = (1, 3)
 ALONG = (5, 7)
 SHARDS = (1, 3, 2, 6, 5, 7)
-RB = 512
-STEPS = ((0,), (4, 8), (1, 3), (2, 6), (5, 7))
+YFIRST = 6
+RB = 1024
+STEPS = ((0,), (4,), (8, 1), (3, 2), (6, 5, 7))
 C = 192.0 ** -0.5 * 1.4426950408889634
 BIG = -1.0e30
 NT = (((1,), (1,)), ((), ()))
@@ -125,9 +126,8 @@
         at = kbuf.at[k, half, :]
         return remote(at, at, ss.at[k], rs.at[k], (sib, tp))
 
-    H2 = HEADS // 2
-
-    lo, hi = pl.ds(0, H2), pl.ds(H2, H2)
+
+    lo, hi = pl.ds(0, YFIRST), pl.ds(YFIRST, HEADS - YFIRST)
 
     def wy1(d):
         return remote(w_hbm.at[lo], wbuf.at[lo, z, y, core], swy.at[0], rwy.at[0], ypeer(d))
@@ -144,7 +144,8 @@
         return remote(at, at, swy.at[1], rwy.at[1], ypeer(d))
 
     def wthree(along_y, stage):
-        at = wbuf.at[lo, pl.ds(0, 3), 0, 0] if stage == 0 else wbuf.at[lo, pl.ds(0, 3), :, 0]
+        heads = lo if along_y == (stage == 0) else hi
+        at = wbuf.at[heads, pl.ds(0, 3), 0, 0] if stage == 0 else wbuf.at[heads, pl.ds(0, 3), :, 0]
         if along_y:
             return remote(at, at, swy.at[stage], rwy.at[stage], ypeer(1))
         return remote(at, at, swz.at[stage], rwz.at[stage], zpeer(1))
@@ -307,10 +308,33 @@
             if i > 0:
                 values(STEPS[i - 1], (i - 1) % 2, r, i == 1, i == len(STEPS))
 
+    def early():
+        xthree(0).wait_send()
+        scopy(0).wait_send()
+        wthree(True, 0).wait_send()
+        wthree(False, 0).wait_send()
+        for r in (1, 2):
+            @pl.when(z + r <= 3)
+            def _():
+                zcopy(r).wait_send()
+
+            @pl.when(z >= r)
+            def _():
+                xthree(4 * r).wait_send()
+                scopy(4 * r).wait_send()
+        for k in SHARDS:
+            @pl.when(yneed(k) & shards(k))
+            def _():
+                ycopy(k, my_rows).wait_send()
+        for k in DIRECT:
+            @pl.when(first & (dp + 2 * k <= 31))
+            def _():
+                bcopy(k).wait_send()
+
     issue(1)
-    issue(3)
     arrive(0)
     step(0)
+    issue(3)
     issue(2)
     issue(6)
     issue(5)
@@ -323,58 +347,41 @@
     along(7, 2)
     weights2()
     arrive(4)
-    arrive(8)
     step(1)
     relay(1)
     relay(3)
+    arrive(8)
     arrive(1)
-    arrive(3)
     step(2)
     relay(2)
     relay(6)
+    early()
     relay(5)
     relay(7)
+    arrive(3)
     arrive(2)
+    step(3)
+    weights4()
+    weights5()
     arrive(6)
-    step(3)
     arrive(5)
     arrive(7)
-    weights4()
     step(4)
-    weights5()
-    step(5)
-
+    wsib(0).wait_recv()
+    wsib(1).wait_recv()
+    step(len(STEPS))
     for h in range(HEADS):
-        if h % H2 == 0:
-            wsib(h // H2).wait_recv()
         wv = wbuf[h].reshape(LATENT, VALUE)
         o_ref[:, h * VALUE:(h + 1) * VALUE] = jnp.dot(ctx[h * TOK:(h + 1) * TOK, :], wv, preferred_element_type=F32).astype(BF16)
-
-    xthree(0).wait_send()
-    for stage in range(2):
-        wthree(True, stage).wait_send()
-        wthree(False, stage).wait_send()
-        wsib(stage).wait_send()
-    for r in (1, 2):
-        @pl.when(z + r <= 3)
-        def _():
-            zcopy(r).wait_send()
-
-    for k in SHARDS:
-        @pl.when(yneed(k) & shards(k))
-        def _():
-            ycopy(k, my_rows).wait_send()
-    for k in DIRECT:
-        @pl.when(first & (dp + 2 * k <= 31))
-        def _():
-            bcopy(k).wait_send()
+    wthree(True, 1).wait_send()
+    wthree(False, 1).wait_send()
+    wsib(0).wait_send()
+    wsib(1).wait_send()
     for k in ALONG:
         @pl.when(first & yneed(k))
         def _():
             ycopy(k, half).wait_send()
-
-    scopy(0).wait_send()
-    for k in range(1, NCH):
+    for k in SHARDS:
         @pl.when(has_src(k))
         def _():
             scopy(k).wait_send()

time: 35.5 us -> 34 us (0.958)
  the two profiles are of different devices: /device:TPU:89 before, /device:TPU:32 now
where the time goes in v4:
time: 34 us; the launch traced here: 33.9 us
  Pallas kernels  33 us (97%)
  local copies, waits for them, and re-layouts  0.8 us (2%)
    pallas_call x1, Pallas kernels, per_device(): pl.pallas_call(kernel, out_shape=pltpu.VMEM((TOK, HEADS * VALUE), BF16),...  33 us
    unnamed x1, local copies, waits for them, and re-layouts  0.8 us

profile of v4, /device:TPU:32, one launch (start us, length us, event | category | flops | bytes accessed | tf_op | source)
XLA Modules:
  0.0 33.9 jit_solution(9826482320094022465)
XLA Ops:
  0.0 33.0 %shard_map.46 = bf16[128,2048]{1,0:T(8,128)(2,1)S(1)} custom-call(bf16[128,9216]{1,0:T(8,128)(2,1)} %q_hbm.1, bf16[32,576]{1,0:T(8,128)(2,1)} %lat_hbm.1, s32[1,128]{1,0:T(1,128)} %bitcast.1, bf16[16,16,128]{2,1,0:T(8,128)(2,1)} %w_hbm.1), custom_call_target="tpu_custom_call" | custom-call | flops 11000000512 | bytes 8000000 | tf_op jit(solution)/shard_map/pallas_call | solution.py:396
  33.1 0.8 %copy.6 = bf16[128,2048]{1,0:T(8,128)(2,1)} copy(bf16[128,2048]{1,0:T(8,128)(2,1)S(1)} %shard_map.46) | data formatting | bytes 1048576

commit v5 on v4

--- a/solution.py
+++ b/solution.py
@@ -224,12 +224,12 @@
 
     def weights2():
         wown.wait()
+        wthree(False, 0).wait_recv()
+        for d in (1, 3, 2):
+            wy2(d).start()
         wthree(True, 0).wait_recv()
         for d in (1, 3, 2):
             wz2(d).start()
-        wthree(False, 0).wait_recv()
-        for d in (1, 3, 2):
-            wy2(d).start()
 
     def weights4():
         wthree(False, 1).wait_recv()
@@ -350,10 +350,11 @@
     step(1)
     relay(1)
     relay(3)
+    relay(2, second)
     arrive(8)
     arrive(1)
     step(2)
-    relay(2)
+    relay(2, first)
     relay(6)
     early()
     relay(5)

time: 34 us -> 33.8 us (level)
  no operation moved by 1% of the time
where the time goes in v5:
time: 33.8 us; the launch traced here: 33.7 us
  Pallas kernels  32.9 us (97%)
  local copies, waits for them, and re-layouts  0.8 us (2%)
    pallas_call x1, Pallas kernels, per_device(): pl.pallas_call(kernel, out_shape=pltpu.VMEM((TOK, HEADS * VALUE), BF16),...  32.9 us
    unnamed x1, local copies, waits for them, and re-layouts  0.8 us

profile of v5, /device:TPU:32, one launch (start us, length us, event | category | flops | bytes accessed | tf_op | source)
XLA Modules:
  0.0 33.7 jit_solution(16639399595927981739)
XLA Ops:
  0.0 32.9 %shard_map.46 = bf16[128,2048]{1,0:T(8,128)(2,1)S(1)} custom-call(bf16[128,9216]{1,0:T(8,128)(2,1)} %q_hbm.1, bf16[32,576]{1,0:T(8,128)(2,1)} %lat_hbm.1, s32[1,128]{1,0:T(1,128)} %bitcast.1, bf16[16,16,128]{2,1,0:T(8,128)(2,1)} %w_hbm.1), custom_call_target="tpu_custom_call" | custom-call | flops 11000000512 | bytes 8000000 | tf_op jit(solution)/shard_map/pallas_call | solution.py:397
  32.9 0.8 %copy.6 = bf16[128,2048]{1,0:T(8,128)(2,1)} copy(bf16[128,2048]{1,0:T(8,128)(2,1)S(1)} %shard_map.46) | data formatting | bytes 1048576

commit v6 on v5

--- a/solution.py
+++ b/solution.py
@@ -225,7 +225,7 @@
     def weights2():
         wown.wait()
         wthree(False, 0).wait_recv()
-        for d in (1, 3, 2):
+        for d in (2, 1, 3):
             wy2(d).start()
         wthree(True, 0).wait_recv()
         for d in (1, 3, 2):

time: 33.8 us -> 34.4 us (1.018)
  the two profiles are of different devices: /device:TPU:32 before, /device:TPU:99 now
where the time goes in v6:
time: 34.4 us; the launch traced here: 34.3 us
  Pallas kernels  33.5 us (97%)
  local copies, waits for them, and re-layouts  0.8 us (2%)
    pallas_call x1, Pallas kernels, per_device(): pl.pallas_call(kernel, out_shape=pltpu.VMEM((TOK, HEADS * VALUE), BF16),...  33.5 us
    unnamed x1, local copies, waits for them, and re-layouts  0.8 us

profile of v6, /device:TPU:99, one launch (start us, length us, event | category | flops | bytes accessed | tf_op | source)
XLA Modules:
  0.0 34.3 jit_solution(6813050081397436307)
XLA Ops:
  0.0 33.5 %shard_map.46 = bf16[128,2048]{1,0:T(8,128)(2,1)S(1)} custom-call(bf16[128,9216]{1,0:T(8,128)(2,1)} %q_hbm.1, bf16[32,576]{1,0:T(8,128)(2,1)} %lat_hbm.1, s32[1,128]{1,0:T(1,128)} %bitcast.1, bf16[16,16,128]{2,1,0:T(8,128)(2,1)} %w_hbm.1), custom_call_target="tpu_custom_call" | custom-call | flops 11000000512 | bytes 8000000 | tf_op jit(solution)/shard_map/pallas_call | solution.py:397
  33.5 0.8 %copy.6 = bf16[128,2048]{1,0:T(8,128)(2,1)} copy(bf16[128,2048]{1,0:T(8,128)(2,1)S(1)} %shard_map.46) | data formatting | bytes 1048576
